TPU v7x, 128 devices: a whole 4x4x4 slice. The times are simulated.
128 devices in a mesh: row: 2 (over core), col: 2 (over x_lo), layer: 32 (over z, y, x_hi).
Axes of the slice: x: 4 (x_hi: 2, x_lo: 2; x = x_hi * 2 + x_lo), y: 4, z: 4, core: 2. Of those that a mesh axis runs over, the one named last changes fastest.
Arguments:
- left: bfloat16 [16384, 65536], P('row', ('layer', 'col'))
- pattern_left: int32 [64, 256], P('row', ('layer', 'col')), may hold values from 0 to 1, as said below
- right: bfloat16 [65536, 1024], P(('layer', 'row'), 'col'), may hold values from -0.0234375 to 0.0234375
- pattern_right: int32 [256, 4], P(('layer', 'row'), 'col'), may hold values from 0 to 1, as said below
- keep: int32 [64, 4], P(('row', 'layer'), 'col'), may hold values from 0 to 1, as said below
Outputs:
- flow: float32 [16384, 1024], P(('row', 'layer'), 'col')
Inputs may be any that keep to these rules, and one draw needn't show every extreme that they name: `pattern_left`: column 0 of tiles is all ones; each tile row has its own share of stored tiles, from 0.2 to 0.8, and in each aligned block of 4 tile columns stores at most 3; tile row 0 stores exactly 3 in every block. `pattern_right`: row 0 of tiles is all ones; each tile column has its own share of stored tiles, from 0.2 to 0.8. `keep`: every tile column keeps the tile in tile row equal to its index modulo 16384 // 256.
All inputs are finite; a program needn't handle non-finite values.
Results may differ from a plain program's by a relative error of at most 0.0003.
Values may be sent and summed in bfloat16 or wider, within the bound.
A program may use at most 320 MiB of HBM per device.

v0:
```python
import jax
import jax.numpy as jnp
from jax import lax
from jax.sharding import PartitionSpec as P


def masked_tiles(values, pattern):
    rows, cols = values.shape
    tile_rows, tile_cols = pattern.shape
    shaped = values.reshape(tile_rows, rows // tile_rows, tile_cols, cols // tile_cols)
    return (shaped * pattern[:, None, :, None].astype(values.dtype)).reshape(rows, cols)


def body(left, pattern_left, right, pattern_right, keep):
    left_all, pattern_all = (
        lax.all_gather(left, "col", axis=1, tiled=True),
        lax.all_gather(pattern_left, "col", axis=1, tiled=True),
    )
    left_kept = masked_tiles(left_all, pattern_all)
    values = lax.all_gather(right, "row", axis=0, tiled=True)
    pattern = lax.all_gather(pattern_right, "row", axis=0, tiled=True)
    panel = masked_tiles(values, pattern)
    partial_value = jnp.dot(left_kept, panel, preferred_element_type=jnp.float32)
    expanded = lax.psum_scatter(partial_value, "layer", scatter_dimension=0, tiled=True)
    inflated = masked_tiles(expanded * expanded, keep)
    totals = lax.psum(jnp.sum(inflated, axis=0), ("row", "layer"))
    scaled = jnp.float32(inflated.shape[0] * lax.axis_size("row") * lax.axis_size("layer"))
    return scaled * inflated / (totals + 1e-06)


def solution(mesh):
    return jax.shard_map(
        body,
        mesh=mesh,
        in_specs=(
            P("row", ("layer", "col")),
            P("row", ("layer", "col")),
            P(("layer", "row"), "col"),
            P(("layer", "row"), "col"),
            P(("row", "layer"), "col"),
        ),
        out_specs=P(("row", "layer"), "col"),
        check_vma=False,
    )
```

profile of v0, /device:TPU:1, one launch (start us, length us, event | category | flops | bytes accessed | tf_op | source)
XLA Modules:
  0.0 990.8 jit_solution(13772862756100712107)
XLA Ops:
  6.5 0.0 copy-start.1
  6.5 0.0 copy-start
  6.5 0.0 all-gather.7.cloned.1.call-start
  6.5 0.7 all-gather.7.cloned.1.call-update
  7.3 0.0 all-gather.5.cloned.1.call-start
  7.3 0.7 all-gather.5.cloned.1.call-update
  8.0 0.0 reduce-scatter.2.cloned.1.call-start
  8.1 0.0 copy-done.1
  8.1 2.9 all-gather.1
  11.0 0.0 copy-done
  11.0 3.2 all-gather
  14.1 0.1 copy.9
  14.2 11.6 %mul.46 = bf16[32,256,8,256]{3,2,1,0:T(8,128)(2,1)} broadcast(bf16[32,8]{1,0:T(8,128)(2,1)S(1)} %copy.9), dimensions={0,2} | broadcast | bytes 33554944 | tf_op jit(solution)/shard_map/mul | solution.py:11
  25.8 27.1 %copy.14 = bf16[1024,8,8,256]{3,1,2,0:T(8,128)(2,1)} copy(bf16[1024,8,8,256]{3,2,1,0:T(8,128)(2,1)} %bitcast.19) | data formatting | bytes 67108864
  52.9 0.1 copy.12
  53.0 1.1 mul.49
  54.2 0.5 copy.15
  54.6 0.0 all-gather.7.cloned.1.call-done
  54.7 365.0 %all-gather.5.cloned.1.call-done = bf16[8192,2048]{1,0:T(8,128)(2,1)} async-done(((bf16[8192,1024]{1,0:T(8,128)(2,1)}), bf16[8192,2048]{1,0:T(8,128)(2,1)}) %all-gather.5.cloned.1.call-update) | async-done | bytes 33554448 | tf_op jit(solution)/shard_map/all_gather | solution.py:16
  419.7 31.1 %fusion = f32[8192,512]{1,0:T(8,128)} fusion(bf16[8192,2048]{1,0:T(8,128)(2,1)} %all-gather.5.cloned.1.call-done, bf16[8192,2048]{1,0:T(8,128)(2,1)} %bitcast.20, bf16[2048,512]{1,0:T(8,128)(2,1)} %all-gather.7.cloned.1.call-done, bf16[2048,512]{1,0:T(8,128)(2,1)S(1)} %bitcast.22), kind=kOutput, calls=%fused_computation | convolution fusion | flops 17197694976 | bytes 88080384 | tf_op jit(solution)/shard_map/dot_general | solution.py:23
  450.7 0.0 copy-start.2
  450.7 0.0 reduce-scatter.2.cloned.1.call-update
  450.7 0.6 copy-done.2
  451.4 0.1 broadcast_bitcast_fusion
  451.5 365.0 %reduce-scatter.2.cloned.1.call-done = f32[256,512]{1,0:T(8,128)} async-done(((f32[8192,512]{1,0:T(8,128)}), f32[256,512]{1,0:T(8,128)}) %reduce-scatter.2.cloned.1.call-update) | async-done | bytes 524304 | tf_op jit(solution)/shard_map/reduce_scatter | solution.py:24
  816.5 1.1 fusion.3
  817.6 164.8 %psum.7 = f32[512]{0:T(512)S(1)} all-reduce(f32[512]{0:T(512)S(1)} %fusion.3), channel_id=1, replica_groups=mesh['row'=2,'col'=2,'layer'=32] {'row','layer'}, use_global_device_ids=true, to_apply=%region_2.0 | all-reduce | flops 512 | bytes 4096 | tf_op jit(solution)/shard_map/psum | solution.py:26
  982.4 1.9 multiply_divide_fusion
  (5 shorter events, 0.0 us)
Async XLA Ops:
  6.5 1.5 copy-start.1
  6.5 4.4 copy-start
  6.5 48.1 %all-gather.7.cloned.1.call-start = ((), (), s32[]{:S(2)}) async-start(), calls=%async_computation.2 | async-start | bytes 3145728 | tf_op jit(solution)/shard_map/all_gather | solution.py:20
  7.3 412.4 %all-gather.5.cloned.1.call-start = ((), (), s32[]{:S(2)}) async-start(), calls=%async_computation.1 | async-start | bytes 50331648 | tf_op jit(solution)/shard_map/all_gather | solution.py:16
  8.0 808.5 %reduce-scatter.2.cloned.1.call-start = ((), (), s32[]{:S(2)}) async-start(), calls=%async_computation.3 | async-start | bytes 17301504 | tf_op jit(solution)/shard_map/reduce_scatter | solution.py:24
  450.7 0.7 copy-start.2
Sparse Core Ops, SparseCore 0:
  9.0 16.9 all-gather.6
  27.6 391.9 all-gather.4
  450.9 365.5 reduce-scatter.1
where the time goes:
time: 991 us
  waiting for transfers between devices  731 us (74%)
  blocking collectives  171 us (17%)
  local copies, waits for them, and re-layouts  41.2 us (4%)
  matrix products  31.1 us (3%)
  between operations  13.1 us (1%)
    reduce_scatter x1, waiting for transfers between devices, body(): lax.psum_scatter(partial_value, 'layer', scatter_dimension=0, tiled=True)  365 us
    all_gather x1, waiting for transfers between devices, body(): lax.all_gather(left, 'col', axis=1, tiled=True)  365 us
    psum x1, blocking collectives, body(): totals = lax.psum(jnp.sum(inflated, axis=0), ('row', 'layer'))  165 us
    dot_general x1, matrix products, body(): jnp.dot(left_kept, panel, preferred_element_type=jnp.float32)  31.1 us
    unnamed x10, local copies, waits for them, and re-layouts  28.3 us
  transfers between devices with their start and end apart: 3, of which 2 were waited for; matrix products, arithmetic and copies ran while one was open for 4% of the time, Pallas kernels for 0%

commit v1 on v0

v1 whole, which is shorter than its diff:
```python
import functools
import math

import jax
import jax.numpy as jnp
from jax import lax
from jax.experimental import pallas as pl
from jax.experimental.pallas import tpu as pltpu
from jax.sharding import PartitionSpec as P

MESH = pl.DeviceIdType.MESH
TILE = 256
DEPTH = 1024
WIDE = 512
HEAD = 16
FINE = 64
TOP = 32700.0
A, B, C = 0, 1, 2
ROWS = (64, 96, 96)
START = (0, 64, 160)
PLAN = (
    ((2, 0), (2, 1), (0, 0), (3, 0), (1, 1), (0, 1), (1, 0), (3, 1)),
    ((2, 0), (3, 0), (0, 0), (2, 1), (1, 1), (0, 1), (1, 0), (3, 1)),
    ((2, 0), (3, 0), (0, 0), (2, 1), (1, 1), (0, 1), (1, 0), (3, 1)),
)
MESSAGES = (((2, 0), 1), ((2, 1), 3), ((3, 0), 3), ((1, 1), 1), ((1, 0), 1), ((3, 1), 3))
MERGED = {4: 0, 5: 1}
OWN = ((2, 4), (3, 5))
RING = ((0, 1, 2), (1, 2, 0), (2, 0, 1))


def place():
    layer = lax.axis_index("layer")
    x = lax.rem(layer, 2) * 2 + lax.axis_index("col")
    return lax.axis_index("row"), (x, lax.rem(layer // 2, 4), layer // 8)


def device(core, xyz):
    x, y, z = xyz
    return (core, lax.rem(x, 2), z * 8 + y * 2 + x // 2)


def moved(xyz, dim, by):
    return tuple(lax.rem(v + by, 4) if d == dim else v for d, v in enumerate(xyz))


def pick(table, index):
    value = jnp.int32(table[-1])
    for k in range(len(table) - 2, -1, -1):
        value = jnp.where(index == k, jnp.int32(table[k]), value)
    return value


def aligned(value, by=16):
    return pl.multiple_of(value, by)


def column_scale(codes):
    return jnp.exp(codes * (math.log(2.0) / FINE))


def encode(acc, segments, rows, out):
    top = jnp.zeros((HEAD, WIDE), jnp.float32)
    for base in segments:
        def look(i, top, base=base):
            return jnp.maximum(top, jnp.abs(acc[pl.ds(aligned(base + i * 16), 16), :]))

        top = lax.fori_loop(0, rows // 16, look, top)
    top = jnp.broadcast_to(jnp.max(top, axis=0, keepdims=True), (HEAD, WIDE))
    codes = jnp.ceil(jnp.log(jnp.maximum(top, 1e-30)) * (FINE / math.log(2.0)))
    out[pl.ds(0, HEAD), :] = codes.astype(jnp.int32).astype(jnp.int16)
    inverse = TOP / column_scale(codes)
    for k, base in enumerate(segments):
        def write(i, _, base=base, k=k):
            value = acc[pl.ds(aligned(base + i * 16), 16), :] * inverse
            out[pl.ds(aligned(HEAD + k * rows + i * 16), 16), :] = (
                jnp.round(value).astype(jnp.int32).astype(jnp.int16)
            )
            return 0

        lax.fori_loop(0, rows // 16, write, 0)


def add(acc, segments, rows, messages):
    scales = [
        column_scale(m[pl.ds(0, HEAD), :].astype(jnp.int32).astype(jnp.float32)) * (1.0 / TOP)
        for m in messages
    ]
    for k, base in enumerate(segments):
        def step(i, _, base=base, k=k):
            at = pl.ds(aligned(base + i * 16), 16)
            value = acc[at, :]
            for m, scale in zip(messages, scales):
                got = m[pl.ds(aligned(HEAD + k * rows + i * 16), 16), :]
                value += got.astype(jnp.int32).astype(jnp.float32) * scale
            acc[at, :] = value
            return 0

        lax.fori_loop(0, rows // 16, step, 0)


def kernel(
    left, pattern_left, right, pattern_right, keep, inflated, totals,
    panel, lefts, accs, send1, recv1, send2, recv2, send3, recv3, tsend, trecv,
    lsem, psend, precv, ssem1, rsem1, ssem2, rsem2, ssem3, rsem3, tssem, trsem,
):
    core, xyz = place()
    x, y, z = xyz
    col = lax.rem(x, 2)
    pair = (x + 1 - 2 * col, y, z)
    mate = device(1 - core, xyz)
    owner = core == col

    def load(part, step):
        by = pick([p[0] for p in PLAN[part]], step)
        half = pick([p[1] for p in PLAN[part]], step)
        rows = pl.ds(START[part], ROWS[part])
        if part == A:
            source = left.at[pl.ds(half * 2, 2), :, lax.rem(x + by, 4) // 2, rows, :]
        elif part == B:
            source = left.at[:, lax.rem(y + by, 4), :, rows, :]
        else:
            source = left.at[lax.rem(z + by, 4), :, :, rows, :]
        return pltpu.make_async_copy(source, lefts[part], lsem.at[part])

    for part in (B, C, A):
        load(part, jnp.int32(0)).start()

    peers = [mate, device(1 - core, pair), device(1 - core, moved(xyz, 0, 2))]
    peers += [device(core, moved(xyz, d, by)) for d in range(3) for by in (1, 2, 3)]
    barrier = pltpu.get_barrier_semaphore()
    for peer in peers:
        pl.semaphore_signal(barrier, inc=1, device_id=peer, device_id_type=MESH)

    slot = jnp.where(owner, 0, 2)
    for k in range(4):
        for j in range(2):
            at = (pl.ds(k * TILE, TILE), pl.ds(j * TILE, TILE))
            mask = jnp.full((TILE, TILE), pattern_right[k, j].astype(jnp.float32))
            panel[(slot,) + at] = right[at] * mask.astype(jnp.bfloat16)
    pl.semaphore_wait(barrier, len(peers))

    HALF = DEPTH // 2

    def share():
        return pltpu.make_async_remote_copy(
            panel.at[0], panel.at[0], psend.at[0], precv.at[0], device_id=mate, device_id_type=MESH
        )

    def export(to):
        rows = pl.ds(to * HALF, HALF)
        return pltpu.make_async_remote_copy(
            panel.at[2, rows], panel.at[1, rows], psend.at[1 + to], precv.at[1],
            device_id=device(jnp.int32(to), pair), device_id_type=MESH,
        )

    def forward():
        rows = pl.ds(aligned(core * HALF), HALF)
        return pltpu.make_async_remote_copy(
            panel.at[1, rows], panel.at[1, rows], psend.at[3], precv.at[2], device_id=mate, device_id_type=MESH
        )

    @pl.when(owner)
    def _():
        share().start()

    @pl.when(jnp.logical_not(owner))
    def _():
        export(0).start()
        export(1).start()
        share().wait_recv()

    def message1(part, k):
        to = device(core, moved(xyz, RING[part][0], MESSAGES[k][1]))
        return pltpu.make_async_remote_copy(
            send1[part].at[k], recv1[part].at[k], ssem1.at[part, k], rsem1.at[part, k],
            device_id=to, device_id_type=MESH,
        )

    def multiply(part, step):
        by = pick([p[0] for p in PLAN[part]], step)
        half = pick([p[1] for p in PLAN[part]], step)
        rows = ROWS[part]
        load(part, step).wait()
        block = lefts[part]
        for a in range(block.shape[0]):
            for b in range(block.shape[1]):
                if part == A:
                    tile = (half * 2 + a) * 8 + b * 2 + lax.rem(x + by, 4) // 2
                elif part == B:
                    tile = a * 8 + lax.rem(y + by, 4) * 2 + b
                else:
                    tile = lax.rem(z + by, 4) * 8 + a * 2 + b
                for k in range(4):
                    at = (a, b, slice(None), pl.ds(k * TILE, TILE))
                    mask = jnp.full((rows, TILE), pattern_left[tile, k].astype(jnp.float32))
                    block[at] = block[at] * mask.astype(jnp.bfloat16)
        columns = lax.rem(by, 2) if part == A else half
        to = jnp.where(by == 0, half, 2)
        accs[part][pl.ds(aligned(to * (8 * rows)), 8 * rows), :] = jnp.dot(
            block[...].reshape(8 * rows, DEPTH), panel[columns], preferred_element_type=jnp.float32
        )

        @pl.when(step < 7)
        def _():
            load(part, step + 1).start()

    def steps(step, _):
        @pl.when(step == 3)
        def _():
            export(0).wait_recv()
            forward().start()
            forward().wait_recv()
            for k in (0, 1):
                message1(A, k).start()

        for part in (B, C, A):
            rows = 8 * ROWS[part]
            multiply(part, step)
            for k, merged in MERGED.items():
                @pl.when(step == PLAN[part].index(MESSAGES[k][0]))
                def _(k=k, merged=merged, part=part, rows=rows):
                    message1(part, merged).wait_recv()
                    add(accs[part], [2 * rows], rows, [recv1[part].at[merged]])

            at = [PLAN[part].index(m[0]) for m in MESSAGES]
            sends = functools.reduce(jnp.logical_or, [step == i for i in at])

            @pl.when(sends)
            def _(part=part, rows=rows, at=at):
                k = sum(jnp.where(step == i, n, 0) for n, i in enumerate(at))
                encode(accs[part], [2 * rows], rows, send1[part].at[k])

            for k, i in enumerate(at):
                if part != A or k > 1:
                    @pl.when(step == i)
                    def _(k=k, part=part):
                        message1(part, k).start()

        return 0

    lax.fori_loop(0, 8, steps, 0)

    def bases2(part, by, half):
        rows = ROWS[part]
        if part == A:
            return [half * (8 * rows) + (a * 4 + lax.rem(y + by, 4)) * rows for a in (0, 1)]
        if part == B:
            return [half * (8 * rows) + (lax.rem(z + by, 4) * 2 + b) * rows for b in (0, 1)]
        return [(by % 2) * (8 * rows) + ((half * 2 + a) * 2 + lax.rem(x + by, 4) // 2) * rows for a in (0, 1)]

    def message2(part, k):
        to = device(core, moved(xyz, RING[part][1], MESSAGES[k][1]))
        return pltpu.make_async_remote_copy(
            send2[part].at[k], recv2[part].at[k], ssem2.at[part, k], rsem2.at[part, k],
            device_id=to, device_id_type=MESH,
        )

    for part in (B, C, A):
        rows = 8 * ROWS[part]
        for half in (0, 1):
            for k in OWN[half]:
                message1(part, k).wait_recv()
            add(accs[part], [half * rows], rows, [recv1[part].at[k] for k in OWN[half]])
        for k in (0, 1, 2, 3):
            encode(accs[part], bases2(part, *MESSAGES[k][0]), ROWS[part], send2[part].at[k])
            message2(part, k).start()
    for part in (B, C, A):
        for k, merged in MERGED.items():
            bases = bases2(part, *MESSAGES[k][0])
            message2(part, merged).wait_recv()
            add(accs[part], bases, ROWS[part], [recv2[part].at[merged]])
            encode(accs[part], bases, ROWS[part], send2[part].at[k])
            message2(part, k).start()

    def base3(part, by):
        rows = ROWS[part]
        if part == A:
            to = lax.rem(z + by, 4)
            return to // 2 * (8 * rows) + (lax.rem(to, 2) * 4 + y) * rows
        if part == B:
            return (by % 2) * (8 * rows) + (z * 2 + lax.rem(x + by, 4) // 2) * rows
        return (lax.rem(y + by, 4) * 2 + x // 2) * rows

    def message3(part, by):
        to = device(core, moved(xyz, RING[part][2], by))
        return pltpu.make_async_remote_copy(
            send3[part].at[by - 1], recv3[part].at[by - 1], ssem3.at[part, by - 1], rsem3.at[part, by - 1],
            device_id=to, device_id_type=MESH,
        )

    for part in (B, C, A):
        for half in (0, 1):
            for k in OWN[half]:
                message2(part, k).wait_recv()
            add(accs[part], bases2(part, 0, half), ROWS[part], [recv2[part].at[k] for k in OWN[half]])
        for by in (2, 1, 3):
            encode(accs[part], [base3(part, by)], ROWS[part], send3[part].at[by - 1])
            message3(part, by).start()

    keeps = [keep[0, j].astype(jnp.float32) for j in range(2)]
    sums = jnp.zeros((16, WIDE), jnp.float32)
    for part in (B, C, A):
        for by in (2, 1, 3):
            message3(part, by).wait_recv()
        add(accs[part], [base3(part, 0)], ROWS[part], [recv3[part].at[by - 1] for by in (2, 1, 3)])
        kept = jnp.concatenate([jnp.full((16, TILE), v) for v in keeps], axis=1)

        def finish(i, sums, part=part, kept=kept):
            value = accs[part][pl.ds(aligned(base3(part, 0) + i * 16), 16), :]
            value = value * value * kept
            inflated[pl.ds(aligned(START[part] + i * 16), 16), :] = value
            return sums + value

        sums = lax.fori_loop(0, ROWS[part] // 16, finish, sums)
    sums = jnp.sum(sums, axis=0, keepdims=True)

    rounds = (
        [mate, device(core, moved(xyz, 0, 2)), device(1 - core, moved(xyz, 0, 2))],
        [device(core, moved(xyz, 1, by)) for by in (1, 2, 3)],
        [device(core, moved(xyz, 2, by)) for by in (1, 2, 3)],
    )
    total = jnp.concatenate([sums[:, k * 128 : (k + 1) * 128] for k in range(4)] + [jnp.zeros((4, 128), jnp.float32)], axis=0)
    copies = []
    for n, group in enumerate(rounds):
        tsend[n] = total
        now = [
            pltpu.make_async_remote_copy(
                tsend.at[n], trecv.at[n, k], tssem.at[n, k], trsem.at[n, k], device_id=peer, device_id_type=MESH
            )
            for k, peer in enumerate(group)
        ]
        for copy in now:
            copy.start()
        for k, copy in enumerate(now):
            copy.wait_recv()
            total = total + trecv[n, k]
        copies += now
    totals[...] = total

    for copy in copies:
        copy.wait_send()
    for part in range(3):
        for k in range(6):
            message1(part, k).wait_send()
            message2(part, k).wait_send()
        for by in (1, 2, 3):
            message3(part, by).wait_send()
    forward().wait_send()

    @pl.when(owner)
    def _():
        share().wait_send()

    @pl.when(jnp.logical_not(owner))
    def _():
        export(0).wait_send()
        export(1).wait_send()


def body(left, pattern_left, right, pattern_right, keep):
    vmem = pl.BlockSpec(memory_space=pltpu.VMEM)
    smem = pl.BlockSpec(memory_space=pltpu.SMEM)
    dma = pltpu.SemaphoreType.DMA
    blocks = [(2, 4), (4, 2), (4, 2)]
    inflated, totals = pl.pallas_call(
        kernel,
        out_shape=(jax.ShapeDtypeStruct((TILE, WIDE), jnp.float32), jax.ShapeDtypeStruct((8, 128), jnp.float32)),
        in_specs=[pl.BlockSpec(memory_space=pl.ANY), smem, vmem, smem, smem],
        out_specs=(vmem, vmem),
        scratch_shapes=[
            pltpu.VMEM((3, DEPTH, WIDE), jnp.bfloat16),
            [pltpu.VMEM(b + (r, DEPTH), jnp.bfloat16) for b, r in zip(blocks, ROWS)],
            [pltpu.VMEM((3 * 8 * r, WIDE), jnp.float32) for r in ROWS],
            [pltpu.VMEM((6, HEAD + 8 * r, WIDE), jnp.int16) for r in ROWS],
            [pltpu.VMEM((6, HEAD + 8 * r, WIDE), jnp.int16) for r in ROWS],
            [pltpu.VMEM((6, HEAD + 2 * r, WIDE), jnp.int16) for r in ROWS],
            [pltpu.VMEM((6, HEAD + 2 * r, WIDE), jnp.int16) for r in ROWS],
            [pltpu.VMEM((3, HEAD + r, WIDE), jnp.int16) for r in ROWS],
            [pltpu.VMEM((3, HEAD + r, WIDE), jnp.int16) for r in ROWS],
            pltpu.VMEM((3, 8, 128), jnp.float32),
            pltpu.VMEM((3, 3, 8, 128), jnp.float32),
            dma((3,)), dma((4,)), dma((3,)), dma((3, 6)), dma((3, 6)), dma((3, 6)), dma((3, 6)),
            dma((3, 3)), dma((3, 3)), dma((3, 3)), dma((3, 3)),
        ],
        compiler_params=pltpu.CompilerParams(
            collective_id=0, has_side_effects=True, vmem_limit_bytes=62 * 1024 * 1024
        ),
        name="expand",
    )(left.reshape(4, 4, 2, TILE, DEPTH), pattern_left, right, pattern_right, keep)
    return jnp.float32(16384) * inflated / (totals[:4].reshape(WIDE) + 1e-6)


def solution(mesh):
    return jax.shard_map(
        body,
        mesh=mesh,
        in_specs=(
            P("row", ("layer", "col")),
            P("row", ("layer", "col")),
            P(("layer", "row"), "col"),
            P(("layer", "row"), "col"),
            P(("row", "layer"), "col"),
        ),
        out_specs=P(("row", "layer"), "col"),
        check_vma=False,
    )
```

time: 991 us -> 117 us (0.12)
  the two profiles are of different devices: /device:TPU:1 before, /device:TPU:2 now
where the time goes in v1:
time: 117 us
  Pallas kernels  112 us (96%)
  local copies, waits for them, and re-layouts  2.7 us (2%)
  other arithmetic  2.59 us (2%)
    pallas_call x1, Pallas kernels, body(): pl.pallas_call(kernel, out_shape=(jax.ShapeDtypeStruct((TILE, WIDE), jnp....  112 us
    unnamed x2, local copies, waits for them, and re-layouts  2.7 us

profile of v1, /device:TPU:2, one launch (start us, length us, event | category | flops | bytes accessed | tf_op | source)
XLA Modules:
  0.0 116.8 jit_solution(15154968732145334216)
XLA Ops:
  0.0 1.3 %copy.7.pattern_right = s32[4,2]{1,0:T(4,128)} copy(s32[4,2]{0,1:T(2,128)} %param.8) | data formatting | bytes 64 | tf_op args[3]
  1.3 1.4 %copy.6.pattern_left = s32[32,4]{1,0:T(8,128)} copy(s32[32,4]{0,1:T(4,128)} %param.6) | data formatting | bytes 1024 | tf_op args[1]
  2.7 111.5 %expand.1 = (f32[256,512]{1,0:T(8,128)}, f32[8,128]{1,0:T(8,128)}) custom-call(bf16[4,4,2,256,1024]{4,3,2,1,0:T(8,128)(2,1)} %bitcast.3, s32[32,4]{1,0:T(8,128)} %copy.6.pattern_left, bf16[1024,512]{1,0:T(8,128)(2,1)} %right.1, s32[4,2]{1,0:T(4,128)} %copy.7.pattern_right, s32[1,2]{1,0:T(1,128)} %keep.1), custom_call_target="tpu_custom_call" | custom-call | tf_op jit(solution)/shard_map/expand/pallas_call | solution.py:366
  114.2 0.7 add_bitcast_fusion
  114.9 1.9 %multiply_divide_fusion = f32[256,512]{1,0:T(8,128)} fusion(f32[256,512]{1,0:T(8,128)} %get-tuple-element.7, f32[512]{0:T(512)S(1)} %add_bitcast_fusion), kind=kLoop, calls=%fused_computation | loop fusion | flops 262144 | bytes 1050624 | tf_op jit(solution)/shard_map/div | solution.py:391

commit v2 on v1

v2 whole, which is shorter than its diff:
```python
import functools
import math

import jax
import jax.numpy as jnp
from jax import lax
from jax.experimental import pallas as pl
from jax.experimental.pallas import tpu as pltpu
from jax.sharding import PartitionSpec as P

MESH = pl.DeviceIdType.MESH
TILE = 256
DEPTH = 1024
WIDE = 512
LANES = 128
GROUPS = WIDE // LANES
HEAD = 16
FINE = 64
TOP = 32700.0
A, B, C = 0, 1, 2
ORDER = (B, C, A)
SUBS = 2
ROWS = (32, 48, 48)
START = (0, 64, 160)
PLAN = (
    ((2, 0), (2, 1), (0, 0), (3, 0), (1, 1), (0, 1), (1, 0), (3, 1)),
    ((2, 0), (3, 0), (0, 0), (2, 1), (1, 1), (0, 1), (1, 0), (3, 1)),
    ((2, 0), (3, 0), (0, 0), (2, 1), (1, 1), (0, 1), (1, 0), (3, 1)),
)
STEPS = len(PLAN[0])
MESSAGES = (((2, 0), 1), ((2, 1), 3), ((3, 0), 3), ((1, 1), 1), ((1, 0), 1), ((3, 1), 3))
MERGED = {4: 0, 5: 1}
OWN = ((2, 4), (3, 5))
RING = ((0, 1, 2), (1, 2, 0), (2, 0, 1))


def place():
    layer = lax.axis_index("layer")
    x = lax.rem(layer, 2) * 2 + lax.axis_index("col")
    return lax.axis_index("row"), (x, lax.rem(layer // 2, 4), layer // 8)


def device(core, xyz):
    x, y, z = xyz
    return (core, lax.rem(x, 2), z * 8 + y * 2 + x // 2)


def moved(xyz, dim, by):
    return tuple(lax.rem(v + by, 4) if d == dim else v for d, v in enumerate(xyz))


def pick(table, index):
    value = jnp.int32(table[-1])
    for k in range(len(table) - 2, -1, -1):
        value = jnp.where(index == k, jnp.int32(table[k]), value)
    return value


def aligned(value, by=16):
    return pl.multiple_of(value, by)


def loop(count, step, init):
    return lax.fori_loop(0, count, step, init, unroll=True if count <= 6 else 4)


def column_scale(codes):
    return jnp.exp(codes * (math.log(2.0) / FINE))


def encode(acc, segments, rows, out):
    top = jnp.zeros((HEAD, WIDE), jnp.float32)
    for base in segments:
        def look(i, top, base=base):
            return jnp.maximum(top, jnp.abs(acc[pl.ds(aligned(base + i * 16), 16), :]))

        top = loop(rows // 16, look, top)
    top = jnp.broadcast_to(jnp.max(top, axis=0, keepdims=True), (HEAD, WIDE))
    codes = jnp.ceil(jnp.log(jnp.maximum(top, 1e-30)) * (FINE / math.log(2.0)))
    row = lax.broadcasted_iota(jnp.int32, (HEAD, LANES), 0)
    head = codes[:, :LANES]
    for g in range(1, GROUPS):
        head = jnp.where(row == g, codes[:, g * LANES : (g + 1) * LANES], head)
    out[pl.ds(0, HEAD), :] = head.astype(jnp.int32).astype(jnp.int16)
    inverse = TOP / column_scale(codes)
    for k, base in enumerate(segments):
        def write(i, _, base=base, k=k):
            value = jnp.round(acc[pl.ds(aligned(base + i * 16), 16), :] * inverse)
            value = value.astype(jnp.int32).astype(jnp.int16)
            for g in range(GROUPS):
                at = HEAD + (g * len(segments) + k) * rows + i * 16
                out[pl.ds(aligned(at), 16), :] = value[:, g * LANES : (g + 1) * LANES]
            return 0

        loop(rows // 16, write, 0)


def add(acc, segments, rows, messages):
    scales = []
    for m in messages:
        head = column_scale(m[pl.ds(0, HEAD), :].astype(jnp.int32).astype(jnp.float32)) * (1.0 / TOP)
        scales.append([jnp.broadcast_to(head[g : g + 1, :], (16, LANES)) for g in range(GROUPS)])
    for k, base in enumerate(segments):
        def step(i, _, base=base, k=k):
            at = pl.ds(aligned(base + i * 16), 16)
            for g in range(GROUPS):
                lanes = pl.ds(g * LANES, LANES)
                value = acc[at, lanes]
                for m, scale in zip(messages, scales):
                    got = m[pl.ds(aligned(HEAD + (g * len(segments) + k) * rows + i * 16), 16), :]
                    value += got.astype(jnp.int32).astype(jnp.float32) * scale[g]
                acc[at, lanes] = value
            return 0

        loop(rows // 16, step, 0)


def kernel(
    left, pattern_left, right, pattern_right, keep, inflated, totals,
    panel, lefts, accs, send1, recv1, send2, recv2, send3, recv3, tsend, trecv,
    lsem, psem, psend, precv, ssem1, rsem1, ssem2, rsem2, ssem3, rsem3, tssem, trsem,
):
    core, xyz = place()
    x, y, z = xyz
    col = lax.rem(x, 2)
    pair = (x + 1 - 2 * col, y, z)
    mate = device(1 - core, xyz)
    owner = core == col
    slot = jnp.where(owner, 0, 2)
    fetch = pltpu.make_async_copy(right, panel.at[slot], psem)
    fetch.start()

    def load(part, step):
        sub, step = step // STEPS, lax.rem(step, STEPS)
        by = pick([p[0] for p in PLAN[part]], step)
        half = pick([p[1] for p in PLAN[part]], step)
        rows = pl.ds(aligned(START[part] + sub * ROWS[part]), ROWS[part])
        if part == A:
            source = left.at[pl.ds(half * 2, 2), :, lax.rem(x + by, 4) // 2, rows, :]
        elif part == B:
            source = left.at[:, lax.rem(y + by, 4), :, rows, :]
        else:
            source = left.at[lax.rem(z + by, 4), :, :, rows, :]
        return pltpu.make_async_copy(source, lefts[part], lsem.at[part])

    for part in ORDER:
        load(part, jnp.int32(0)).start()

    rounds = (
        [mate] + [device(c, moved(xyz, 1, by)) for by in (1, 2, 3) for c in (core, 1 - core)],
        [device(core, moved(xyz, 0, 2))]
        + [device(core, moved(moved(xyz, 2, by), 0, dx)) for by in (1, 2, 3) for dx in (0, 2)],
    )
    peers = [p for group in rounds for p in group]
    peers += [device(1 - core, pair), device(core, moved(xyz, 0, 1)), device(core, moved(xyz, 0, 3))]
    barrier = pltpu.get_barrier_semaphore()
    for peer in peers:
        pl.semaphore_signal(barrier, inc=1, device_id=peer, device_id_type=MESH)

    fetch.wait()
    for k in range(4):
        for j in range(2):
            at = (slot, pl.ds(k * TILE, TILE), pl.ds(j * TILE, TILE))
            mask = jnp.full((TILE, TILE), pattern_right[j, k].astype(jnp.float32))
            panel[at] = panel[at] * mask.astype(jnp.bfloat16)
    pl.semaphore_wait(barrier, len(peers))

    HALF = DEPTH // 2

    def share():
        return pltpu.make_async_remote_copy(
            panel.at[0], panel.at[0], psend.at[0], precv.at[0], device_id=mate, device_id_type=MESH
        )

    def export(to):
        rows = pl.ds(to * HALF, HALF)
        return pltpu.make_async_remote_copy(
            panel.at[2, rows], panel.at[1, rows], psend.at[1 + to], precv.at[1],
            device_id=device(jnp.int32(to), pair), device_id_type=MESH,
        )

    def forward():
        rows = pl.ds(aligned(core * HALF), HALF)
        return pltpu.make_async_remote_copy(
            panel.at[1, rows], panel.at[1, rows], psend.at[3], precv.at[2], device_id=mate, device_id_type=MESH
        )

    @pl.when(owner)
    def _():
        share().start()

    @pl.when(jnp.logical_not(owner))
    def _():
        export(0).start()
        export(1).start()
        share().wait_recv()

    def message(ring, part, sub, k):
        send, recv, ssem, rsem = (
            (send1, recv1, ssem1, rsem1),
            (send2, recv2, ssem2, rsem2),
            (send3, recv3, ssem3, rsem3),
        )[ring]
        count, by = (3, k + 1) if ring == 2 else (6, MESSAGES[k][1])
        n = sub * count + k
        return pltpu.make_async_remote_copy(
            send[part].at[n], recv[part].at[n], ssem.at[part, n], rsem.at[part, n],
            device_id=device(core, moved(xyz, RING[part][ring], by)), device_id_type=MESH,
        )

    def base1(part, sub, half):
        return (sub * 2 + half) * (8 * ROWS[part])

    WORK = SUBS * 2 * 8

    def multiply(part, step, sub, i):
        by = pick([p[0] for p in PLAN[part]], i)
        half = pick([p[1] for p in PLAN[part]], i)
        rows = ROWS[part]
        load(part, step).wait()
        block = lefts[part]
        for a in range(block.shape[0]):
            for b in range(block.shape[1]):
                if part == A:
                    tile = (half * 2 + a) * 8 + b * 2 + lax.rem(x + by, 4) // 2
                elif part == B:
                    tile = a * 8 + lax.rem(y + by, 4) * 2 + b
                else:
                    tile = lax.rem(z + by, 4) * 8 + a * 2 + b
                for k in range(4):
                    at = (a, b, slice(None), pl.ds(k * TILE, TILE))
                    mask = jnp.full((rows, TILE), pattern_left[k, tile].astype(jnp.float32))
                    block[at] = block[at] * mask.astype(jnp.bfloat16)
        columns = lax.rem(by, 2) if part == A else half
        to = jnp.where(by == 0, base1(part, sub, half), WORK * rows)
        accs[part][pl.ds(aligned(to), 8 * rows), :] = jnp.dot(
            block[...].reshape(8 * rows, DEPTH), panel[columns], preferred_element_type=jnp.float32
        )

        @pl.when(step < SUBS * STEPS - 1)
        def _():
            load(part, step + 1).start()

    def bases2(part, sub, by, half):
        rows = ROWS[part]
        if part == A:
            return [base1(part, sub, half) + (a * 4 + lax.rem(y + by, 4)) * rows for a in (0, 1)]
        if part == B:
            return [base1(part, sub, half) + (lax.rem(z + by, 4) * 2 + b) * rows for b in (0, 1)]
        at = [(half * 2 + a) * 2 + lax.rem(x + by, 4) // 2 for a in (0, 1)]
        return [base1(part, sub, by % 2) + a * rows for a in at]

    def base3(part, sub, by):
        rows = ROWS[part]
        if part == A:
            to = lax.rem(z + by, 4)
            return base1(part, sub, to // 2) + (lax.rem(to, 2) * 4 + y) * rows
        if part == B:
            return base1(part, sub, by % 2) + (z * 2 + lax.rem(x + by, 4) // 2) * rows
        return base1(part, sub, 0) + (lax.rem(y + by, 4) * 2 + x // 2) * rows

    def second_first(sub):
        for part in ORDER:
            for half in (0, 1):
                for k in OWN[half]:
                    message(0, part, sub, k).wait_recv()
                got = [recv1[part].at[sub * 6 + k] for k in OWN[half]]
                add(accs[part], [base1(part, sub, half)], 8 * ROWS[part], got)
            for k in (0, 1, 2, 3):
                encode(accs[part], bases2(part, sub, *MESSAGES[k][0]), ROWS[part], send2[part].at[sub * 6 + k])
                message(1, part, sub, k).start()

    def second_merge(sub):
        for part in ORDER:
            for k, merged in MERGED.items():
                bases = bases2(part, sub, *MESSAGES[k][0])
                message(1, part, sub, merged).wait_recv()
                add(accs[part], bases, ROWS[part], [recv2[part].at[sub * 6 + merged]])
                encode(accs[part], bases, ROWS[part], send2[part].at[sub * 6 + k])
                message(1, part, sub, k).start()

    def third(sub):
        for part in ORDER:
            for half in (0, 1):
                for k in OWN[half]:
                    message(1, part, sub, k).wait_recv()
                got = [recv2[part].at[sub * 6 + k] for k in OWN[half]]
                add(accs[part], bases2(part, sub, 0, half), ROWS[part], got)
            for by in (2, 1, 3):
                encode(accs[part], [base3(part, sub, by)], ROWS[part], send3[part].at[sub * 3 + by - 1])
                message(2, part, sub, by - 1).start()

    keeps = [keep[0, j].astype(jnp.float32) for j in range(2)]
    kept = jnp.concatenate([jnp.full((16, TILE), v) for v in keeps], axis=1)

    def finish(sub, sums):
        for part in ORDER:
            for by in (2, 1, 3):
                message(2, part, sub, by - 1).wait_recv()
            base = base3(part, sub, 0)
            add(accs[part], [base], ROWS[part], [recv3[part].at[sub * 3 + by - 1] for by in (2, 1, 3)])
            for i in range(ROWS[part] // 16):
                value = accs[part][pl.ds(aligned(base + i * 16), 16), :]
                value = value * value * kept
                inflated[pl.ds(START[part] + sub * ROWS[part] + i * 16, 16), :] = value
                sums = sums + value
        return sums

    def steps(step, _):
        sub, i = step // STEPS, lax.rem(step, STEPS)

        @pl.when(step == 3)
        def _():
            export(0).wait_recv()
            forward().start()
            forward().wait_recv()
            for k in (0, 1):
                message(0, A, 0, k).start()

        @pl.when(step == STEPS + 6)
        def _():
            second_first(0)

        for part in ORDER:
            rows = 8 * ROWS[part]
            work = WORK * ROWS[part]
            multiply(part, step, sub, i)
            for k, merged in MERGED.items():
                @pl.when(i == PLAN[part].index(MESSAGES[k][0]))
                def _(merged=merged, part=part, rows=rows, work=work):
                    message(0, part, sub, merged).wait_recv()
                    add(accs[part], [work], rows, [recv1[part].at[sub * 6 + merged]])

            at = [PLAN[part].index(m[0]) for m in MESSAGES]

            @pl.when(functools.reduce(jnp.logical_or, [i == j for j in at]))
            def _(part=part, rows=rows, at=at, work=work):
                k = sum(jnp.where(i == j, n, 0) for n, j in enumerate(at))
                encode(accs[part], [work], rows, send1[part].at[sub * 6 + k])

            for k, j in enumerate(at):
                now = i == j
                if part == A and k < 2:
                    now = jnp.logical_and(now, sub > 0)

                @pl.when(now)
                def _(k=k, part=part):
                    message(0, part, sub, k).start()

        return 0

    lax.fori_loop(0, SUBS * STEPS, steps, 0)
    sums = jnp.zeros((16, WIDE), jnp.float32)
    second_merge(0)
    second_first(1)
    third(0)
    second_merge(1)
    sums = finish(0, sums)
    third(1)
    sums = finish(1, sums)
    sums = jnp.sum(sums, axis=0, keepdims=True)

    parts = [sums[:, g * LANES : (g + 1) * LANES] for g in range(GROUPS)]
    total = jnp.concatenate(parts + [jnp.zeros((8 - GROUPS, LANES), jnp.float32)], axis=0)
    copies = []
    for n, group in enumerate(rounds):
        tsend[n] = total
        now = [
            pltpu.make_async_remote_copy(
                tsend.at[n], trecv.at[n, k], tssem.at[n, k], trsem.at[n, k], device_id=peer, device_id_type=MESH
            )
            for k, peer in enumerate(group)
        ]
        for copy in now:
            copy.start()
        for k, copy in enumerate(now):
            copy.wait_recv()
            total = total + trecv[n, k]
        copies += now
    for g in range(GROUPS):
        totals[:, pl.ds(g * LANES, LANES)] = total[g : g + 1, :] + 1e-6

    for copy in copies:
        copy.wait_send()
    for part in range(3):
        for sub in range(SUBS):
            for k in range(6):
                message(0, part, sub, k).wait_send()
                message(1, part, sub, k).wait_send()
            for k in range(3):
                message(2, part, sub, k).wait_send()
    forward().wait_send()

    @pl.when(owner)
    def _():
        share().wait_send()

    @pl.when(jnp.logical_not(owner))
    def _():
        export(0).wait_send()
        export(1).wait_send()


def body(left, pattern_left, right, pattern_right, keep):
    vmem = pl.BlockSpec(memory_space=pltpu.VMEM)
    smem = pl.BlockSpec(memory_space=pltpu.SMEM)
    hbm = pl.BlockSpec(memory_space=pl.ANY)
    dma = pltpu.SemaphoreType.DMA
    blocks = [(2, 4), (4, 2), (4, 2)]

    def buffers(count, pieces):
        return [
            pltpu.VMEM((SUBS * count, HEAD + GROUPS * pieces * r, LANES), jnp.int16) for r in ROWS
        ]

    inflated, totals = pl.pallas_call(
        kernel,
        out_shape=(jax.ShapeDtypeStruct((TILE, WIDE), jnp.float32), jax.ShapeDtypeStruct((1, WIDE), jnp.float32)),
        in_specs=[hbm, smem, hbm, smem, smem],
        out_specs=(vmem, vmem),
        scratch_shapes=[
            pltpu.VMEM((3, DEPTH, WIDE), jnp.bfloat16),
            [pltpu.VMEM(b + (r, DEPTH), jnp.bfloat16) for b, r in zip(blocks, ROWS)],
            [pltpu.VMEM(((SUBS * 2 + 1) * 8 * r, WIDE), jnp.float32) for r in ROWS],
            buffers(6, 8), buffers(6, 8), buffers(6, 2), buffers(6, 2), buffers(3, 1), buffers(3, 1),
            pltpu.VMEM((2, 8, LANES), jnp.float32),
            pltpu.VMEM((2, 7, 8, LANES), jnp.float32),
            dma((3,)), dma, dma((4,)), dma((3,)), dma((3, SUBS * 6)), dma((3, SUBS * 6)),
            dma((3, SUBS * 6)), dma((3, SUBS * 6)), dma((3, SUBS * 3)), dma((3, SUBS * 3)), dma((2, 7)), dma((2, 7)),
        ],
        compiler_params=pltpu.CompilerParams(
            collective_id=0, has_side_effects=True, vmem_limit_bytes=60 * 1024 * 1024
        ),
        name="expand",
    )(left.reshape(4, 4, 2, TILE, DEPTH), pattern_left.T, right, pattern_right.T, keep)
    return jnp.float32(16384) * inflated / totals


def solution(mesh):
    return jax.shard_map(
        body,
        mesh=mesh,
        in_specs=(
            P("row", ("layer", "col")),
            P("row", ("layer", "col")),
            P(("layer", "row"), "col"),
            P(("layer", "row"), "col"),
            P(("row", "layer"), "col"),
        ),
        out_specs=P(("row", "layer"), "col"),
        check_vma=False,
    )
```

time: 117 us -> 105 us (0.90)
  the two profiles are of different devices: /device:TPU:2 before, /device:TPU:1 now
where the time goes in v2:
time: 105 us
  Pallas kernels  103 us (98%)
  other arithmetic  1.92 us (2%)
    pallas_call x1, Pallas kernels, body(): pl.pallas_call(kernel, out_shape=(jax.ShapeDtypeStruct((TILE, WIDE), jnp....  103 us

profile of v2, /device:TPU:1, one launch (start us, length us, event | category | flops | bytes accessed | tf_op | source)
XLA Modules:
  0.0 105.2 jit_solution(9450823417007009386)
XLA Ops:
  0.0 103.3 %expand.1 = (f32[256,512]{1,0:T(8,128)}, f32[1,512]{1,0:T(1,128)}) custom-call(bf16[4,4,2,256,1024]{4,3,2,1,0:T(8,128)(2,1)} %bitcast.4, s32[4,32]{1,0:T(4,128)} %bitcast.5, bf16[1024,512]{1,0:T(8,128)(2,1)} %right.1, s32[2,4]{1,0:T(2,128)} %bitcast.7, s32[1,2]{1,0:T(1,128)} %keep.1), custom_call_target="tpu_custom_call" | custom-call | tf_op jit(solution)/shard_map/expand/pallas_call | solution.py:416
  103.3 1.9 %multiply_divide_fusion = f32[256,512]{1,0:T(8,128)} fusion(f32[256,512]{1,0:T(8,128)} %get-tuple-element.7, f32[512]{0:T(512)} %bitcast.6), kind=kLoop, calls=%fused_computation | loop fusion | flops 262144 | bytes 1050624 | tf_op jit(solution)/shard_map/div | solution.py:436

commit v3 on v2

--- a/solution.py
+++ b/solution.py
@@ -1,4 +1,3 @@
-import functools
 import math
 
 import jax
@@ -22,12 +21,17 @@
 SUBS = 2
 ROWS = (32, 48, 48)
 START = (0, 64, 160)
-PLAN = (
-    ((2, 0), (2, 1), (0, 0), (3, 0), (1, 1), (0, 1), (1, 0), (3, 1)),
-    ((2, 0), (3, 0), (0, 0), (2, 1), (1, 1), (0, 1), (1, 0), (3, 1)),
-    ((2, 0), (3, 0), (0, 0), (2, 1), (1, 1), (0, 1), (1, 0), (3, 1)),
+PLAN_A = (
+    (0, 2, 0), (0, 2, 1), (1, 2, 0), (1, 2, 1), (0, 0, 0), (1, 0, 0), (0, 0, 1), (0, 3, 0),
+    (0, 1, 1), (0, 1, 0), (0, 3, 1), (1, 3, 0), (1, 1, 1), (1, 1, 0), (1, 3, 1), (1, 0, 1),
 )
-STEPS = len(PLAN[0])
+PLAN_BC = (
+    (0, 2, 0), (0, 3, 0), (1, 2, 0), (1, 3, 0), (0, 0, 0), (1, 0, 0), (0, 1, 0), (0, 2, 1),
+    (1, 2, 1), (0, 1, 1), (1, 1, 1), (1, 1, 0), (0, 0, 1), (0, 3, 1), (1, 0, 1), (1, 3, 1),
+)
+PLAN = (PLAN_A, PLAN_BC, PLAN_BC)
+STEPS = len(PLAN_A)
+EARLY, WHOLE = 5, 7
 MESSAGES = (((2, 0), 1), ((2, 1), 3), ((3, 0), 3), ((1, 1), 1), ((1, 0), 1), ((3, 1), 3))
 MERGED = {4: 0, 5: 1}
 OWN = ((2, 4), (3, 5))
@@ -118,7 +122,7 @@
 def kernel(
     left, pattern_left, right, pattern_right, keep, inflated, totals,
     panel, lefts, accs, send1, recv1, send2, recv2, send3, recv3, tsend, trecv,
-    lsem, psem, psend, precv, ssem1, rsem1, ssem2, rsem2, ssem3, rsem3, tssem, trsem,
+    lsem, psem, psend, precv, ssem1, rsem1, ssem2, rsem2, ssem3, rsem3, tssem, trsem, late,
 ):
     core, xyz = place()
     x, y, z = xyz
@@ -130,10 +134,11 @@
     fetch = pltpu.make_async_copy(right, panel.at[slot], psem)
     fetch.start()
 
+    def now(part, step):
+        return [pick([p[n] for p in PLAN[part]], step) for n in range(3)]
+
     def load(part, step):
-        sub, step = step // STEPS, lax.rem(step, STEPS)
-        by = pick([p[0] for p in PLAN[part]], step)
-        half = pick([p[1] for p in PLAN[part]], step)
+        sub, by, half = now(part, step)
         rows = pl.ds(aligned(START[part] + sub * ROWS[part]), ROWS[part])
         if part == A:
             source = left.at[pl.ds(half * 2, 2), :, lax.rem(x + by, 4) // 2, rows, :]
@@ -151,8 +156,7 @@
         [device(core, moved(xyz, 0, 2))]
         + [device(core, moved(moved(xyz, 2, by), 0, dx)) for by in (1, 2, 3) for dx in (0, 2)],
     )
-    peers = [p for group in rounds for p in group]
-    peers += [device(1 - core, pair), device(core, moved(xyz, 0, 1)), device(core, moved(xyz, 0, 3))]
+    peers = [mate, device(1 - core, pair)] + [device(core, moved(xyz, d, by)) for d in range(3) for by in (1, 3)]
     barrier = pltpu.get_barrier_semaphore()
     for peer in peers:
         pl.semaphore_signal(barrier, inc=1, device_id=peer, device_id_type=MESH)
@@ -166,23 +170,25 @@
     pl.semaphore_wait(barrier, len(peers))
 
     HALF = DEPTH // 2
+    PIECES = 2
 
     def share():
         return pltpu.make_async_remote_copy(
             panel.at[0], panel.at[0], psend.at[0], precv.at[0], device_id=mate, device_id_type=MESH
         )
 
-    def export(to):
-        rows = pl.ds(to * HALF, HALF)
+    def export(to, piece):
+        rows = pl.ds(to * HALF + piece * (HALF // PIECES), HALF // PIECES)
         return pltpu.make_async_remote_copy(
-            panel.at[2, rows], panel.at[1, rows], psend.at[1 + to], precv.at[1],
+            panel.at[2, rows], panel.at[1, rows], psend.at[1 + to * PIECES + piece], precv.at[1 + piece],
             device_id=device(jnp.int32(to), pair), device_id_type=MESH,
         )
 
-    def forward():
-        rows = pl.ds(aligned(core * HALF), HALF)
+    def forward(piece):
+        rows = pl.ds(aligned(core * HALF + piece * (HALF // PIECES)), HALF // PIECES)
         return pltpu.make_async_remote_copy(
-            panel.at[1, rows], panel.at[1, rows], psend.at[3], precv.at[2], device_id=mate, device_id_type=MESH
+            panel.at[1, rows], panel.at[1, rows], psend.at[1 + (2 + piece) + PIECES], precv.at[1 + PIECES + piece],
+            device_id=mate, device_id_type=MESH,
         )
 
     @pl.when(owner)
@@ -191,8 +197,9 @@
 
     @pl.when(jnp.logical_not(owner))
     def _():
-        export(0).start()
-        export(1).start()
+        for piece in range(PIECES):
+            for to in (0, 1):
+                export(to, piece).start()
         share().wait_recv()
 
     def message(ring, part, sub, k):
@@ -213,9 +220,8 @@
 
     WORK = SUBS * 2 * 8
 
-    def multiply(part, step, sub, i):
-        by = pick([p[0] for p in PLAN[part]], i)
-        half = pick([p[1] for p in PLAN[part]], i)
+    def multiply(part, step):
+        sub, by, half = now(part, step)
         rows = ROWS[part]
         load(part, step).wait()
         block = lefts[part]
@@ -237,7 +243,7 @@
             block[...].reshape(8 * rows, DEPTH), panel[columns], preferred_element_type=jnp.float32
         )
 
-        @pl.when(step < SUBS * STEPS - 1)
+        @pl.when(step < STEPS - 1)
         def _():
             load(part, step + 1).start()
 
@@ -307,56 +313,71 @@
         return sums
 
     def steps(step, _):
-        sub, i = step // STEPS, lax.rem(step, STEPS)
-
-        @pl.when(step == 3)
+        @pl.when(step == EARLY)
         def _():
-            export(0).wait_recv()
-            forward().start()
-            forward().wait_recv()
-            for k in (0, 1):
-                message(0, A, 0, k).start()
-
-        @pl.when(step == STEPS + 6)
+            export(0, 0).wait_recv()
+            forward(0).start()
+
+        @pl.when(step == WHOLE)
         def _():
-            second_first(0)
+            export(0, 1).wait_recv()
+            forward(1).start()
+
+            @pl.when(col == 0)
+            def _():
+                for sub in range(SUBS):
+                    message(0, A, sub, 0).start()
+
+            @pl.when(col == 1)
+            def _():
+                for sub in range(SUBS):
+                    message(0, A, sub, 1).start()
+
+            for piece in range(PIECES):
+                forward(piece).wait_recv()
 
         for part in ORDER:
             rows = 8 * ROWS[part]
             work = WORK * ROWS[part]
-            multiply(part, step, sub, i)
+            multiply(part, step)
+            sub, by, half = now(part, step)
+
+            def is_message(k, by=by, half=half):
+                return jnp.logical_and(by == MESSAGES[k][0][0], half == MESSAGES[k][0][1])
+
             for k, merged in MERGED.items():
-                @pl.when(i == PLAN[part].index(MESSAGES[k][0]))
-                def _(merged=merged, part=part, rows=rows, work=work):
+                @pl.when(is_message(k))
+                def _(merged=merged, part=part, rows=rows, work=work, sub=sub):
                     message(0, part, sub, merged).wait_recv()
                     add(accs[part], [work], rows, [recv1[part].at[sub * 6 + merged]])
 
-            at = [PLAN[part].index(m[0]) for m in MESSAGES]
-
-            @pl.when(functools.reduce(jnp.logical_or, [i == j for j in at]))
-            def _(part=part, rows=rows, at=at, work=work):
-                k = sum(jnp.where(i == j, n, 0) for n, j in enumerate(at))
+            @pl.when(by > 0)
+            def _(part=part, rows=rows, work=work, sub=sub):
+                k = sum(jnp.where(is_message(n), n, 0) for n in range(6))
                 encode(accs[part], [work], rows, send1[part].at[sub * 6 + k])
 
-            for k, j in enumerate(at):
-                now = i == j
+            for k in range(6):
+                ready = is_message(k)
                 if part == A and k < 2:
-                    now = jnp.logical_and(now, sub > 0)
-
-                @pl.when(now)
-                def _(k=k, part=part):
+                    ready = jnp.logical_and(ready, col == 1 - k)
+
+                @pl.when(ready)
+                def _(k=k, part=part, sub=sub):
                     message(0, part, sub, k).start()
 
         return 0
 
-    lax.fori_loop(0, SUBS * STEPS, steps, 0)
+    lax.fori_loop(0, STEPS, steps, 0)
     sums = jnp.zeros((16, WIDE), jnp.float32)
+    second_first(0)
+    pl.semaphore_signal(late, inc=1, device_id=mate, device_id_type=MESH)
+    second_first(1)
     second_merge(0)
-    second_first(1)
+    second_merge(1)
     third(0)
-    second_merge(1)
+    third(1)
     sums = finish(0, sums)
-    third(1)
+    pl.semaphore_wait(late, 1)
     sums = finish(1, sums)
     sums = jnp.sum(sums, axis=0, keepdims=True)
 
@@ -389,7 +410,8 @@
                 message(1, part, sub, k).wait_send()
             for k in range(3):
                 message(2, part, sub, k).wait_send()
-    forward().wait_send()
+    for piece in range(PIECES):
+        forward(piece).wait_send()
 
     @pl.when(owner)
     def _():
@@ -397,8 +419,9 @@
 
     @pl.when(jnp.logical_not(owner))
     def _():
-        export(0).wait_send()
-        export(1).wait_send()
+        for piece in range(PIECES):
+            for to in (0, 1):
+                export(to, piece).wait_send()
 
 
 def body(left, pattern_left, right, pattern_right, keep):
@@ -425,8 +448,9 @@
             buffers(6, 8), buffers(6, 8), buffers(6, 2), buffers(6, 2), buffers(3, 1), buffers(3, 1),
             pltpu.VMEM((2, 8, LANES), jnp.float32),
             pltpu.VMEM((2, 7, 8, LANES), jnp.float32),
-            dma((3,)), dma, dma((4,)), dma((3,)), dma((3, SUBS * 6)), dma((3, SUBS * 6)),
+            dma((3,)), dma, dma((7,)), dma((5,)), dma((3, SUBS * 6)), dma((3, SUBS * 6)),
             dma((3, SUBS * 6)), dma((3, SUBS * 6)), dma((3, SUBS * 3)), dma((3, SUBS * 3)), dma((2, 7)), dma((2, 7)),
+            pltpu.SemaphoreType.REGULAR,
         ],
         compiler_params=pltpu.CompilerParams(
             collective_id=0, has_side_effects=True, vmem_limit_bytes=60 * 1024 * 1024

time: 105 us -> 98.4 us (0.937)
  Pallas kernels: 103 us -> 96.3 us
    pallas_call x1, Pallas kernels: 103 us -> 96.3 us  [body(): pl.pallas_call(kernel, out_shape=(jax.ShapeDtypeStruct((TILE, WIDE), jnp....]
where the time goes in v3:
time: 98.4 us; the launch traced here: 98.2 us
  Pallas kernels  96.3 us (98%)
  other arithmetic  1.92 us (2%)
    pallas_call x1, Pallas kernels, body(): pl.pallas_call(kernel, out_shape=(jax.ShapeDtypeStruct((TILE, WIDE), jnp....  96.3 us

profile of v3, /device:TPU:1, one launch (start us, length us, event | category | flops | bytes accessed | tf_op | source)
XLA Modules:
  0.0 98.2 jit_solution(14392003686852143765)
XLA Ops:
  0.0 96.3 %expand.1 = (f32[256,512]{1,0:T(8,128)}, f32[1,512]{1,0:T(1,128)}) custom-call(bf16[4,4,2,256,1024]{4,3,2,1,0:T(8,128)(2,1)} %bitcast.4, s32[4,32]{1,0:T(4,128)} %bitcast.5, bf16[1024,512]{1,0:T(8,128)(2,1)} %right.1, s32[2,4]{1,0:T(2,128)} %bitcast.7, s32[1,2]{1,0:T(1,128)} %keep.1), custom_call_target="tpu_custom_call" | custom-call | tf_op jit(solution)/shard_map/expand/pallas_call | solution.py:439
  96.3 1.9 %multiply_divide_fusion = f32[256,512]{1,0:T(8,128)} fusion(f32[256,512]{1,0:T(8,128)} %get-tuple-element.7, f32[512]{0:T(512)} %bitcast.6), kind=kLoop, calls=%fused_computation | loop fusion | flops 262144 | bytes 1050624 | tf_op jit(solution)/shard_map/div | solution.py:460

commit v4 on v3

--- a/solution.py
+++ b/solution.py
@@ -18,6 +18,8 @@
 TOP = 32700.0
 A, B, C = 0, 1, 2
 ORDER = (B, C, A)
+LAG = 3
+FIRST = ((C, 0), (B, 0), (A, LAG))
 SUBS = 2
 ROWS = (32, 48, 48)
 START = (0, 64, 160)
@@ -34,7 +36,7 @@
 EARLY, WHOLE = 5, 7
 MESSAGES = (((2, 0), 1), ((2, 1), 3), ((3, 0), 3), ((1, 1), 1), ((1, 0), 1), ((3, 1), 3))
 MERGED = {4: 0, 5: 1}
-OWN = ((2, 4), (3, 5))
+OWN = (2, 4)
 RING = ((0, 1, 2), (1, 2, 0), (2, 0, 1))
 
 
@@ -72,57 +74,67 @@
     return jnp.exp(codes * (math.log(2.0) / FINE))
 
 
-def encode(acc, segments, rows, out):
-    top = jnp.zeros((HEAD, WIDE), jnp.float32)
-    for base in segments:
-        def look(i, top, base=base):
-            return jnp.maximum(top, jnp.abs(acc[pl.ds(aligned(base + i * 16), 16), :]))
-
-        top = loop(rows // 16, look, top)
-    top = jnp.broadcast_to(jnp.max(top, axis=0, keepdims=True), (HEAD, WIDE))
+def decoder(sources, rows):
+    scales = []
+    for m, _, _ in sources:
+        head = column_scale(m[pl.ds(0, HEAD), :].astype(jnp.int32).astype(jnp.float32)) * (1.0 / TOP)
+        scales.append([jnp.broadcast_to(head[g : g + 1, :], (16, LANES)) for g in range(GROUPS)])
+
+    def read(value, g, k, i):
+        for (m, stride, begins), scale in zip(sources, scales):
+            got = m[pl.ds(aligned(HEAD + g * stride + begins[k] + i * 16), 16), :]
+            value += got.astype(jnp.int32).astype(jnp.float32) * scale[g]
+        return value
+
+    return read
+
+
+def summed(acc, segments, rows, sources, use, init):
+    read = decoder(sources, rows)
+    for k, base in enumerate(segments):
+        def step(i, carry, base=base, k=k):
+            at = pl.ds(aligned(base + i * 16), 16)
+            if sources:
+                groups = [pl.ds(g * LANES, LANES) for g in range(GROUPS)]
+                value = jnp.concatenate([read(acc[at, lanes], g, k, i) for g, lanes in enumerate(groups)], axis=1)
+            else:
+                value = acc[at, :]
+            return use(at, value, k, i, carry)
+
+        init = loop(rows // 16, step, init)
+    return init
+
+
+def encode(acc, segments, rows, out, sources=()):
+    def look(at, value, k, i, top):
+        if sources:
+            acc[at, :] = value
+        return jnp.maximum(top, jnp.abs(value))
+
+    top = summed(acc, segments, rows, sources, look, jnp.zeros((HEAD, WIDE), jnp.float32))
+    top = jnp.max(top, axis=0, keepdims=True)
     codes = jnp.ceil(jnp.log(jnp.maximum(top, 1e-30)) * (FINE / math.log(2.0)))
     row = lax.broadcasted_iota(jnp.int32, (HEAD, LANES), 0)
-    head = codes[:, :LANES]
-    for g in range(1, GROUPS):
+    head = jnp.zeros((HEAD, LANES), jnp.float32)
+    for g in range(GROUPS):
         head = jnp.where(row == g, codes[:, g * LANES : (g + 1) * LANES], head)
     out[pl.ds(0, HEAD), :] = head.astype(jnp.int32).astype(jnp.int16)
-    inverse = TOP / column_scale(codes)
-    for k, base in enumerate(segments):
-        def write(i, _, base=base, k=k):
-            value = jnp.round(acc[pl.ds(aligned(base + i * 16), 16), :] * inverse)
-            value = value.astype(jnp.int32).astype(jnp.int16)
-            for g in range(GROUPS):
-                at = HEAD + (g * len(segments) + k) * rows + i * 16
-                out[pl.ds(aligned(at), 16), :] = value[:, g * LANES : (g + 1) * LANES]
-            return 0
-
-        loop(rows // 16, write, 0)
-
-
-def add(acc, segments, rows, messages):
-    scales = []
-    for m in messages:
-        head = column_scale(m[pl.ds(0, HEAD), :].astype(jnp.int32).astype(jnp.float32)) * (1.0 / TOP)
-        scales.append([jnp.broadcast_to(head[g : g + 1, :], (16, LANES)) for g in range(GROUPS)])
-    for k, base in enumerate(segments):
-        def step(i, _, base=base, k=k):
-            at = pl.ds(aligned(base + i * 16), 16)
-            for g in range(GROUPS):
-                lanes = pl.ds(g * LANES, LANES)
-                value = acc[at, lanes]
-                for m, scale in zip(messages, scales):
-                    got = m[pl.ds(aligned(HEAD + (g * len(segments) + k) * rows + i * 16), 16), :]
-                    value += got.astype(jnp.int32).astype(jnp.float32) * scale[g]
-                acc[at, lanes] = value
-            return 0
-
-        loop(rows // 16, step, 0)
+    inverse = jnp.broadcast_to(TOP / column_scale(codes), (HEAD, WIDE))
+
+    def write(at, value, k, i, _):
+        value = jnp.round(value * inverse).astype(jnp.int32).astype(jnp.int16)
+        for g in range(GROUPS):
+            to = HEAD + (g * len(segments) + k) * rows + i * 16
+            out[pl.ds(aligned(to), 16), :] = value[:, g * LANES : (g + 1) * LANES]
+        return 0
+
+    summed(acc, segments, rows, (), write, 0)
 
 
 def kernel(
-    left, pattern_left, right, pattern_right, keep, inflated, totals,
-    panel, lefts, accs, send1, recv1, send2, recv2, send3, recv3, tsend, trecv,
-    lsem, psem, psend, precv, ssem1, rsem1, ssem2, rsem2, ssem3, rsem3, tssem, trsem, late,
+    left, pattern_left_in, right, pattern_right_in, keep_in, inflated_out, totals,
+    pattern_left, pattern_right, keep, inflated, panel, lefts, accs, send1, recv1, send2, recv2, send3, recv3, tsend, trecv,
+    msem, osem, lsem, psem, psend, precv, ssem1, rsem1, ssem2, rsem2, ssem3, rsem3, tssem, trsem, late,
 ):
     core, xyz = place()
     x, y, z = xyz
@@ -130,6 +142,18 @@
     pair = (x + 1 - 2 * col, y, z)
     mate = device(1 - core, xyz)
     owner = core == col
+    peers = [mate, device(1 - core, pair)] + [device(core, moved(xyz, d, by)) for d in range(3) for by in (1, 3)]
+    barrier = pltpu.get_barrier_semaphore()
+    for peer in peers:
+        pl.semaphore_signal(barrier, inc=1, device_id=peer, device_id_type=MESH)
+
+    small = [
+        pltpu.make_async_copy(pattern_right_in, pattern_right, msem.at[0]),
+        pltpu.make_async_copy(pattern_left_in, pattern_left, msem.at[1]),
+        pltpu.make_async_copy(keep_in, keep, msem.at[2]),
+    ]
+    for copy in small:
+        copy.start()
     slot = jnp.where(owner, 0, 2)
     fetch = pltpu.make_async_copy(right, panel.at[slot], psem)
     fetch.start()
@@ -151,16 +175,8 @@
     for part in ORDER:
         load(part, jnp.int32(0)).start()
 
-    rounds = (
-        [mate] + [device(c, moved(xyz, 1, by)) for by in (1, 2, 3) for c in (core, 1 - core)],
-        [device(core, moved(xyz, 0, 2))]
-        + [device(core, moved(moved(xyz, 2, by), 0, dx)) for by in (1, 2, 3) for dx in (0, 2)],
-    )
-    peers = [mate, device(1 - core, pair)] + [device(core, moved(xyz, d, by)) for d in range(3) for by in (1, 3)]
-    barrier = pltpu.get_barrier_semaphore()
-    for peer in peers:
-        pl.semaphore_signal(barrier, inc=1, device_id=peer, device_id_type=MESH)
-
+    for copy in small:
+        copy.wait()
     fetch.wait()
     for k in range(4):
         for j in range(2):
@@ -247,70 +263,125 @@
         def _():
             load(part, step + 1).start()
 
-    def bases2(part, sub, by, half):
-        rows = ROWS[part]
+    def pieces2(part, by, half):
         if part == A:
-            return [base1(part, sub, half) + (a * 4 + lax.rem(y + by, 4)) * rows for a in (0, 1)]
+            return half, [a * 4 + lax.rem(y + by, 4) for a in (0, 1)]
         if part == B:
-            return [base1(part, sub, half) + (lax.rem(z + by, 4) * 2 + b) * rows for b in (0, 1)]
-        at = [(half * 2 + a) * 2 + lax.rem(x + by, 4) // 2 for a in (0, 1)]
-        return [base1(part, sub, by % 2) + a * rows for a in at]
-
-    def base3(part, sub, by):
-        rows = ROWS[part]
+            return half, [lax.rem(z + by, 4) * 2 + b for b in (0, 1)]
+        return by % 2, [(half * 2 + a) * 2 + lax.rem(x + by, 4) // 2 for a in (0, 1)]
+
+    def piece3(part, by):
         if part == A:
             to = lax.rem(z + by, 4)
-            return base1(part, sub, to // 2) + (lax.rem(to, 2) * 4 + y) * rows
+            return to // 2, lax.rem(to, 2) * 4 + y, to // 2, lax.rem(to, 2)
         if part == B:
-            return base1(part, sub, by % 2) + (z * 2 + lax.rem(x + by, 4) // 2) * rows
-        return base1(part, sub, 0) + (lax.rem(y + by, 4) * 2 + x // 2) * rows
+            to = lax.rem(x + by, 4) // 2
+            return by % 2, z * 2 + to, by % 2, to
+        to = lax.rem(y + by, 4)
+        return 0, to * 2 + x // 2, to // 2, lax.rem(to, 2)
+
+    def first_sources(part, sub, half, pieces):
+        begins = [p * ROWS[part] for p in pieces]
+        return [(recv1[part].at[sub * 6 + k + half], 8 * ROWS[part], begins) for k in OWN]
+
+    def second(part, sub, k, sources):
+        half, pieces = pieces2(part, *MESSAGES[k][0])
+        segments = [base1(part, sub, half) + p * ROWS[part] for p in pieces]
+        sources = first_sources(part, sub, half, pieces) + sources
+        encode(accs[part], segments, ROWS[part], send2[part].at[sub * 6 + k], sources)
+        message(1, part, sub, k).start()
 
     def second_first(sub):
         for part in ORDER:
-            for half in (0, 1):
-                for k in OWN[half]:
-                    message(0, part, sub, k).wait_recv()
-                got = [recv1[part].at[sub * 6 + k] for k in OWN[half]]
-                add(accs[part], [base1(part, sub, half)], 8 * ROWS[part], got)
-            for k in (0, 1, 2, 3):
-                encode(accs[part], bases2(part, sub, *MESSAGES[k][0]), ROWS[part], send2[part].at[sub * 6 + k])
-                message(1, part, sub, k).start()
+            for k in (2, 3, 4, 5):
+                message(0, part, sub, k).wait_recv()
+            for k in (0, 1):
+                second(part, sub, k, [])
+        for part in ORDER:
+            for k in (2, 3):
+                second(part, sub, k, [])
 
     def second_merge(sub):
         for part in ORDER:
             for k, merged in MERGED.items():
-                bases = bases2(part, sub, *MESSAGES[k][0])
                 message(1, part, sub, merged).wait_recv()
-                add(accs[part], bases, ROWS[part], [recv2[part].at[sub * 6 + merged]])
-                encode(accs[part], bases, ROWS[part], send2[part].at[sub * 6 + k])
-                message(1, part, sub, k).start()
+                rows = ROWS[part]
+                second(part, sub, k, [(recv2[part].at[sub * 6 + merged], 2 * rows, [0, rows])])
+
+    def third_sources(part, sub, by):
+        half, piece, half2, place2 = piece3(part, by)
+        base = base1(part, sub, half) + piece * ROWS[part]
+        sources = first_sources(part, sub, half, [piece])
+        sources += [(recv2[part].at[sub * 6 + k + half2], 2 * ROWS[part], [place2 * ROWS[part]]) for k in OWN]
+        return base, sources
 
     def third(sub):
         for part in ORDER:
-            for half in (0, 1):
-                for k in OWN[half]:
-                    message(1, part, sub, k).wait_recv()
-                got = [recv2[part].at[sub * 6 + k] for k in OWN[half]]
-                add(accs[part], bases2(part, sub, 0, half), ROWS[part], got)
+            for k in (2, 3, 4, 5):
+                message(1, part, sub, k).wait_recv()
             for by in (2, 1, 3):
-                encode(accs[part], [base3(part, sub, by)], ROWS[part], send3[part].at[sub * 3 + by - 1])
+                base, sources = third_sources(part, sub, by)
+                encode(accs[part], [base], ROWS[part], send3[part].at[sub * 3 + by - 1], sources)
                 message(2, part, sub, by - 1).start()
 
     keeps = [keep[0, j].astype(jnp.float32) for j in range(2)]
     kept = jnp.concatenate([jnp.full((16, TILE), v) for v in keeps], axis=1)
 
+    def result(part, sub):
+        at = pl.ds(START[part] + sub * ROWS[part], ROWS[part])
+        return pltpu.make_async_copy(inflated.at[at], inflated_out.at[at], osem.at[part, sub])
+
     def finish(sub, sums):
         for part in ORDER:
+            base, sources = third_sources(part, sub, 0)
             for by in (2, 1, 3):
                 message(2, part, sub, by - 1).wait_recv()
-            base = base3(part, sub, 0)
-            add(accs[part], [base], ROWS[part], [recv3[part].at[sub * 3 + by - 1] for by in (2, 1, 3)])
-            for i in range(ROWS[part] // 16):
-                value = accs[part][pl.ds(aligned(base + i * 16), 16), :]
+                sources.append((recv3[part].at[sub * 3 + by - 1], ROWS[part], [0]))
+
+            def use(at, value, k, i, sums, part=part):
                 value = value * value * kept
-                inflated[pl.ds(START[part] + sub * ROWS[part] + i * 16, 16), :] = value
-                sums = sums + value
+                inflated[pl.ds(aligned(START[part] + sub * ROWS[part] + i * 16), 16), :] = value
+                return sums + value
+
+            sums = summed(accs[part], [base], ROWS[part], sources, use, sums)
+            result(part, sub).start()
         return sums
+
+    def turn(part, step):
+        rows = 8 * ROWS[part]
+        work = WORK * ROWS[part]
+        multiply(part, step)
+        sub, by, half = now(part, step)
+
+        def is_message(k, by=by, half=half):
+            return jnp.logical_and(by == MESSAGES[k][0][0], half == MESSAGES[k][0][1])
+
+        out = sum(jnp.where(is_message(n), n, 0) for n in range(6))
+        merges = jnp.logical_or(is_message(4), is_message(5))
+
+        @pl.when(merges)
+        def _(part=part, rows=rows, work=work, sub=sub, out=out):
+            merged = sub * 6 + jnp.where(out == 4, MERGED[4], MERGED[5])
+            for k, m in MERGED.items():
+                @pl.when(out == k)
+                def _(m=m):
+                    message(0, part, sub, m).wait_recv()
+
+            source = (recv1[part].at[merged], rows, [0])
+            encode(accs[part], [work], rows, send1[part].at[sub * 6 + out], [source])
+
+        @pl.when(jnp.logical_and(by > 0, jnp.logical_not(merges)))
+        def _(part=part, rows=rows, work=work, sub=sub, out=out):
+            encode(accs[part], [work], rows, send1[part].at[sub * 6 + out])
+
+        for k in range(6):
+            ready = is_message(k)
+            if part == A and k < 2:
+                ready = jnp.logical_and(ready, col == 1 - k)
+
+            @pl.when(ready)
+            def _(k=k, part=part, sub=sub):
+                message(0, part, sub, k).start()
 
     def steps(step, _):
         @pl.when(step == EARLY)
@@ -336,38 +407,14 @@
             for piece in range(PIECES):
                 forward(piece).wait_recv()
 
-        for part in ORDER:
-            rows = 8 * ROWS[part]
-            work = WORK * ROWS[part]
-            multiply(part, step)
-            sub, by, half = now(part, step)
-
-            def is_message(k, by=by, half=half):
-                return jnp.logical_and(by == MESSAGES[k][0][0], half == MESSAGES[k][0][1])
-
-            for k, merged in MERGED.items():
-                @pl.when(is_message(k))
-                def _(merged=merged, part=part, rows=rows, work=work, sub=sub):
-                    message(0, part, sub, merged).wait_recv()
-                    add(accs[part], [work], rows, [recv1[part].at[sub * 6 + merged]])
-
-            @pl.when(by > 0)
-            def _(part=part, rows=rows, work=work, sub=sub):
-                k = sum(jnp.where(is_message(n), n, 0) for n in range(6))
-                encode(accs[part], [work], rows, send1[part].at[sub * 6 + k])
-
-            for k in range(6):
-                ready = is_message(k)
-                if part == A and k < 2:
-                    ready = jnp.logical_and(ready, col == 1 - k)
-
-                @pl.when(ready)
-                def _(k=k, part=part, sub=sub):
-                    message(0, part, sub, k).start()
+        for part, behind in FIRST:
+            @pl.when(jnp.logical_and(step >= behind, step < behind + STEPS))
+            def _(part=part, behind=behind):
+                turn(part, step - behind)
 
         return 0
 
-    lax.fori_loop(0, STEPS, steps, 0)
+    lax.fori_loop(0, STEPS + LAG, steps, 0)
     sums = jnp.zeros((16, WIDE), jnp.float32)
     second_first(0)
     pl.semaphore_signal(late, inc=1, device_id=mate, device_id_type=MESH)
@@ -381,6 +428,11 @@
     sums = finish(1, sums)
     sums = jnp.sum(sums, axis=0, keepdims=True)
 
+    rounds = (
+        [mate] + [device(c, moved(xyz, 1, by)) for by in (1, 2, 3) for c in (core, 1 - core)],
+        [device(core, moved(xyz, 0, 2))]
+        + [device(core, moved(moved(xyz, 2, by), 0, dx)) for by in (1, 2, 3) for dx in (0, 2)],
+    )
     parts = [sums[:, g * LANES : (g + 1) * LANES] for g in range(GROUPS)]
     total = jnp.concatenate(parts + [jnp.zeros((8 - GROUPS, LANES), jnp.float32)], axis=0)
     copies = []
@@ -405,6 +457,7 @@
         copy.wait_send()
     for part in range(3):
         for sub in range(SUBS):
+            result(part, sub).wait()
             for k in range(6):
                 message(0, part, sub, k).wait_send()
                 message(1, part, sub, k).wait_send()
@@ -426,7 +479,6 @@
 
 def body(left, pattern_left, right, pattern_right, keep):
     vmem = pl.BlockSpec(memory_space=pltpu.VMEM)
-    smem = pl.BlockSpec(memory_space=pltpu.SMEM)
     hbm = pl.BlockSpec(memory_space=pl.ANY)
     dma = pltpu.SemaphoreType.DMA
     blocks = [(2, 4), (4, 2), (4, 2)]
@@ -439,16 +491,18 @@
     inflated, totals = pl.pallas_call(
         kernel,
         out_shape=(jax.ShapeDtypeStruct((TILE, WIDE), jnp.float32), jax.ShapeDtypeStruct((1, WIDE), jnp.float32)),
-        in_specs=[hbm, smem, hbm, smem, smem],
-        out_specs=(vmem, vmem),
+        in_specs=[hbm] * 5,
+        out_specs=(hbm, vmem),
         scratch_shapes=[
+            pltpu.SMEM((4, 32), jnp.int32), pltpu.SMEM((2, 4), jnp.int32), pltpu.SMEM((1, 2), jnp.int32),
+            pltpu.VMEM((TILE, WIDE), jnp.float32),
             pltpu.VMEM((3, DEPTH, WIDE), jnp.bfloat16),
             [pltpu.VMEM(b + (r, DEPTH), jnp.bfloat16) for b, r in zip(blocks, ROWS)],
             [pltpu.VMEM(((SUBS * 2 + 1) * 8 * r, WIDE), jnp.float32) for r in ROWS],
             buffers(6, 8), buffers(6, 8), buffers(6, 2), buffers(6, 2), buffers(3, 1), buffers(3, 1),
             pltpu.VMEM((2, 8, LANES), jnp.float32),
             pltpu.VMEM((2, 7, 8, LANES), jnp.float32),
-            dma((3,)), dma, dma((7,)), dma((5,)), dma((3, SUBS * 6)), dma((3, SUBS * 6)),
+            dma((3,)), dma((3, SUBS)), dma((3,)), dma, dma((7,)), dma((5,)), dma((3, SUBS * 6)), dma((3, SUBS * 6)),
             dma((3, SUBS * 6)), dma((3, SUBS * 6)), dma((3, SUBS * 3)), dma((3, SUBS * 3)), dma((2, 7)), dma((2, 7)),
             pltpu.SemaphoreType.REGULAR,
         ],

time: 98.4 us -> 95.4 us (0.970)
  Pallas kernels: 96.3 us -> 93.2 us
    pallas_call x1, Pallas kernels: 96.3 us -> 93.2 us  [body(): pl.pallas_call(kernel, out_shape=(jax.ShapeDtypeStruct((TILE, WIDE), jnp....]
where the time goes in v4:
time: 95.4 us; the launch traced here: 95.1 us
  Pallas kernels  93.2 us (98%)
  other arithmetic  1.92 us (2%)
    pallas_call x1, Pallas kernels, body(): pl.pallas_call(kernel, out_shape=(jax.ShapeDtypeStruct((TILE, WIDE), jnp....  93.2 us
    div x1, other arithmetic, body(): return jnp.float32(16384) * inflated / totals  1.92 us

profile of v4, /device:TPU:1, one launch (start us, length us, event | category | flops | bytes accessed | tf_op | source)
XLA Modules:
  0.0 95.1 jit_solution(7022436103616458830)
XLA Ops:
  0.0 93.2 %expand.1 = (f32[256,512]{1,0:T(8,128)}, f32[1,512]{1,0:T(1,128)}) custom-call(bf16[4,4,2,256,1024]{4,3,2,1,0:T(8,128)(2,1)} %bitcast.4, s32[4,32]{1,0:T(4,128)} %bitcast.5, bf16[1024,512]{1,0:T(8,128)(2,1)} %right.1, s32[2,4]{1,0:T(2,128)} %bitcast.7, s32[1,2]{1,0:T(1,128)} %keep_in.1), custom_call_target="tpu_custom_call" | custom-call | tf_op jit(solution)/shard_map/expand/pallas_call | solution.py:491
  93.2 1.9 %multiply_divide_fusion = f32[256,512]{1,0:T(8,128)} fusion(f32[256,512]{1,0:T(8,128)} %get-tuple-element.7, f32[512]{0:T(512)} %bitcast.6), kind=kLoop, calls=%fused_computation | loop fusion | flops 262144 | bytes 1050624 | tf_op jit(solution)/shard_map/div | solution.py:514

commit v5 on v4

--- a/solution.py
+++ b/solution.py
@@ -37,7 +37,7 @@
 MESSAGES = (((2, 0), 1), ((2, 1), 3), ((3, 0), 3), ((1, 1), 1), ((1, 0), 1), ((3, 1), 3))
 MERGED = {4: 0, 5: 1}
 OWN = (2, 4)
-RING = ((0, 1, 2), (1, 2, 0), (2, 0, 1))
+RING = (((0, 2, 1), (1, 0, 2), (2, 1, 0)), ((0, 1, 2), (1, 2, 0), (2, 0, 1)))
 
 
 def place():
@@ -228,7 +228,7 @@
         n = sub * count + k
         return pltpu.make_async_remote_copy(
             send[part].at[n], recv[part].at[n], ssem.at[part, n], rsem.at[part, n],
-            device_id=device(core, moved(xyz, RING[part][ring], by)), device_id_type=MESH,
+            device_id=device(core, moved(xyz, RING[sub if ring else 0][part][ring], by)), device_id_type=MESH,
         )
 
     def base1(part, sub, half):
@@ -263,21 +263,26 @@
         def _():
             load(part, step + 1).start()
 
-    def pieces2(part, by, half):
+    def pieces2(part, sub, by, half):
+        axis = RING[sub][part][1]
+        to = lax.rem(xyz[axis] + by, 4)
+        if part == A and axis == 1:
+            return half, [a * 4 + to for a in (0, 1)]
         if part == A:
-            return half, [a * 4 + lax.rem(y + by, 4) for a in (0, 1)]
-        if part == B:
-            return half, [lax.rem(z + by, 4) * 2 + b for b in (0, 1)]
-        return by % 2, [(half * 2 + a) * 2 + lax.rem(x + by, 4) // 2 for a in (0, 1)]
-
-    def piece3(part, by):
+            return to // 2, [lax.rem(to, 2) * 4 + half * 2 + a for a in (0, 1)]
+        if axis == 0:
+            return by % 2, [(half * 2 + a) * 2 + to // 2 for a in (0, 1)]
+        return half, [to * 2 + b for b in (0, 1)]
+
+    def piece3(part, sub, by):
+        axis = RING[sub][part][2]
+        to = lax.rem(xyz[axis] + by, 4)
+        if part == A and axis == 2:
+            return to // 2, lax.rem(to, 2) * 4 + y, to // 2, lax.rem(to, 2)
         if part == A:
-            to = lax.rem(z + by, 4)
-            return to // 2, lax.rem(to, 2) * 4 + y, to // 2, lax.rem(to, 2)
-        if part == B:
-            to = lax.rem(x + by, 4) // 2
-            return by % 2, z * 2 + to, by % 2, to
-        to = lax.rem(y + by, 4)
+            return z // 2, lax.rem(z, 2) * 4 + to, to // 2, lax.rem(to, 2)
+        if axis == 0:
+            return by % 2, xyz[RING[sub][part][1]] * 2 + to // 2, by % 2, to // 2
         return 0, to * 2 + x // 2, to // 2, lax.rem(to, 2)
 
     def first_sources(part, sub, half, pieces):
@@ -285,7 +290,7 @@
         return [(recv1[part].at[sub * 6 + k + half], 8 * ROWS[part], begins) for k in OWN]
 
     def second(part, sub, k, sources):
-        half, pieces = pieces2(part, *MESSAGES[k][0])
+        half, pieces = pieces2(part, sub, *MESSAGES[k][0])
         segments = [base1(part, sub, half) + p * ROWS[part] for p in pieces]
         sources = first_sources(part, sub, half, pieces) + sources
         encode(accs[part], segments, ROWS[part], send2[part].at[sub * 6 + k], sources)
@@ -309,7 +314,7 @@
                 second(part, sub, k, [(recv2[part].at[sub * 6 + merged], 2 * rows, [0, rows])])
 
     def third_sources(part, sub, by):
-        half, piece, half2, place2 = piece3(part, by)
+        half, piece, half2, place2 = piece3(part, sub, by)
         base = base1(part, sub, half) + piece * ROWS[part]
         sources = first_sources(part, sub, half, [piece])
         sources += [(recv2[part].at[sub * 6 + k + half2], 2 * ROWS[part], [place2 * ROWS[part]]) for k in OWN]

time: 95.4 us -> 94.6 us (level)
  no operation moved by 1% of the time
where the time goes in v5:
time: 94.6 us; the launch traced here: 94.3 us
  Pallas kernels  92.4 us (98%)
  other arithmetic  1.92 us (2%)
    pallas_call x1, Pallas kernels, body(): pl.pallas_call(kernel, out_shape=(jax.ShapeDtypeStruct((TILE, WIDE), jnp....  92.4 us
    div x1, other arithmetic, body(): return jnp.float32(16384) * inflated / totals  1.92 us

profile of v5, /device:TPU:1, one launch (start us, length us, event | category | flops | bytes accessed | tf_op | source)
XLA Modules:
  0.0 94.3 jit_solution(12712381033111794120)
XLA Ops:
  0.0 92.4 %expand.1 = (f32[256,512]{1,0:T(8,128)}, f32[1,512]{1,0:T(1,128)}) custom-call(bf16[4,4,2,256,1024]{4,3,2,1,0:T(8,128)(2,1)} %bitcast.4, s32[4,32]{1,0:T(4,128)} %bitcast.5, bf16[1024,512]{1,0:T(8,128)(2,1)} %right.1, s32[2,4]{1,0:T(2,128)} %bitcast.7, s32[1,2]{1,0:T(1,128)} %keep_in.1), custom_call_target="tpu_custom_call" | custom-call | tf_op jit(solution)/shard_map/expand/pallas_call | solution.py:496
  92.4 1.9 %multiply_divide_fusion = f32[256,512]{1,0:T(8,128)} fusion(f32[256,512]{1,0:T(8,128)} %get-tuple-element.7, f32[512]{0:T(512)} %bitcast.6), kind=kLoop, calls=%fused_computation | loop fusion | flops 262144 | bytes 1050624 | tf_op jit(solution)/shard_map/div | solution.py:519

commit v6 on v5

--- a/solution.py
+++ b/solution.py
@@ -67,7 +67,7 @@
 
 
 def loop(count, step, init):
-    return lax.fori_loop(0, count, step, init, unroll=True if count <= 6 else 4)
+    return lax.fori_loop(0, count, step, init, unroll=True if count <= 6 else 8)
 
 
 def column_scale(codes):
@@ -142,10 +142,14 @@
     pair = (x + 1 - 2 * col, y, z)
     mate = device(1 - core, xyz)
     owner = core == col
-    peers = [mate, device(1 - core, pair)] + [device(core, moved(xyz, d, by)) for d in range(3) for by in (1, 3)]
+    peers = [device(1 - core, pair)] + [device(core, moved(xyz, d, by)) for d in range(3) for by in (1, 3)] + [mate]
     barrier = pltpu.get_barrier_semaphore()
     for peer in peers:
         pl.semaphore_signal(barrier, inc=1, device_id=peer, device_id_type=MESH)
+
+    slot = jnp.where(owner, 0, 2)
+    fetch = pltpu.make_async_copy(right, panel.at[slot], psem)
+    fetch.start()
 
     small = [
         pltpu.make_async_copy(pattern_right_in, pattern_right, msem.at[0]),
@@ -154,10 +158,6 @@
     ]
     for copy in small:
         copy.start()
-    slot = jnp.where(owner, 0, 2)
-    fetch = pltpu.make_async_copy(right, panel.at[slot], psem)
-    fetch.start()
-
     def now(part, step):
         return [pick([p[n] for p in PLAN[part]], step) for n in range(3)]
 

time: 94.6 us -> 94.6 us (level)
  no operation moved by 1% of the time
where the time goes in v6:
time: 94.6 us; the launch traced here: 94.4 us
  Pallas kernels  92.4 us (98%)
  other arithmetic  1.92 us (2%)
    pallas_call x1, Pallas kernels, body(): pl.pallas_call(kernel, out_shape=(jax.ShapeDtypeStruct((TILE, WIDE), jnp....  92.4 us
    div x1, other arithmetic, body(): return jnp.float32(16384) * inflated / totals  1.92 us

profile of v6, /device:TPU:1, one launch (start us, length us, event | category | flops | bytes accessed | tf_op | source)
XLA Modules:
  0.0 94.4 jit_solution(15354888483889794155)
XLA Ops:
  0.0 92.4 %expand.1 = (f32[256,512]{1,0:T(8,128)}, f32[1,512]{1,0:T(1,128)}) custom-call(bf16[4,4,2,256,1024]{4,3,2,1,0:T(8,128)(2,1)} %bitcast.4, s32[4,32]{1,0:T(4,128)} %bitcast.5, bf16[1024,512]{1,0:T(8,128)(2,1)} %right.1, s32[2,4]{1,0:T(2,128)} %bitcast.7, s32[1,2]{1,0:T(1,128)} %keep_in.1), custom_call_target="tpu_custom_call" | custom-call | tf_op jit(solution)/shard_map/expand/pallas_call | solution.py:496
  92.5 1.9 %multiply_divide_fusion = f32[256,512]{1,0:T(8,128)} fusion(f32[256,512]{1,0:T(8,128)} %get-tuple-element.7, f32[512]{0:T(512)} %bitcast.6), kind=kLoop, calls=%fused_computation | loop fusion | flops 262144 | bytes 1050624 | tf_op jit(solution)/shard_map/div | solution.py:519
